TPU v7x, 128 devices: a whole 4x4x4 slice. The times are simulated.
128 devices in a mesh: section: 2 (over core), seq: 4 (over x), wa: 16 (over z, y).
Axes of the slice: x: 4, y: 4, z: 4, core: 2. Of those that a mesh axis runs over, the one named last changes fastest.
Arguments:
- tokens: bfloat16 [4, 1024, 1024], P(None, 'seq'), may hold values from -6 to 6
- cotangent: float32 [4, 1024, 1024], P(None, 'seq'), may hold values from -6 to 6
- in_weight: bfloat16 [2, 1024, 3, 1024], P('section', None, None, 'wa'), may hold values from -0.1875 to 0.1875
- conv_weight: float32 [2, 3, 1024], P('section', None, 'wa'), may hold values from -3 to 3
- out_weight: bfloat16 [2, 1024, 1024], P('section', 'wa'), may hold values from -0.1875 to 0.1875
- norm_gain: float32 [2, 1024], P('section'), may hold values from 0.25 to 1.75
- gate_up_weight: bfloat16 [2, 1024, 2, 4608], P('section', None, None, 'wa'), may hold values from -0.1875 to 0.1875
- down_weight: bfloat16 [2, 4608, 1024], P('section', 'wa'), may hold values from -0.09375 to 0.09375
Outputs:
- layer_out: bfloat16 [2, 4, 1024, 1024], P('section', None, ('seq', 'wa'))
- input_grad: float32 [2, 4, 1024, 1024], P('section', None, ('seq', 'wa'))
- in_weight_grad: float32 [2, 1024, 3, 1024], P('section', None, None, 'wa')
- conv_weight_grad: float32 [2, 3, 1024], P('section', None, 'wa')
- out_weight_grad: float32 [2, 1024, 1024], P('section', 'wa')
- norm_gain_grad: float32 [2, 1024], P('section')
- gate_up_grad: float32 [2, 1024, 2, 4608], P('section', None, None, 'wa')
- down_grad: float32 [2, 4608, 1024], P('section', 'wa')
All inputs are finite; a program needn't handle non-finite values.
Results may differ from a plain program's by a relative error of at most 0.025.
Values may be sent and summed in bfloat16 or wider, within the bound.
A program may use at most 128 MiB of HBM per device.

v0:
```python
import jax
import jax.numpy as jnp
from jax import lax
from jax.sharding import PartitionSpec as P

EPSILON = 1e-05


def passed_along(block, axis, distance):
    devices = range(lax.axis_size(axis))
    route = [((i - distance) % len(devices), i) for i in devices]
    return lax.ppermute(block, axis, route)


def shifted(block, axis, distance):
    devices = range(lax.axis_size(axis))
    route = [(i - distance, i) for i in devices if i - distance in devices]
    return lax.ppermute(block, axis, route)


def contract_first(lhs_matrix, rhs_matrix):
    return lax.dot_general(
        lhs_matrix, rhs_matrix, (((0,), (0,)), ((), ())), preferred_element_type=jnp.float32
    )


def contract_last(lhs_matrix, rhs_matrix):
    return lax.dot_general(
        lhs_matrix, rhs_matrix, (((1,), (1,)), ((), ())), preferred_element_type=jnp.float32
    )


def silu_parts(gate_val):
    sigmoid_val = jax.nn.sigmoid(gate_val)
    return (gate_val * sigmoid_val, sigmoid_val * (1.0 + gate_val * (1.0 - sigmoid_val)))


def body(
    tokens, cotangent, in_weight, conv_weight, out_weight, norm_gain, gate_up_weight, down_weight
):
    micro_count, block_rows, model_width = tokens.shape
    section_index = lax.axis_index("section")
    seq_index = lax.axis_index("seq")
    seq_count = lax.axis_size("seq")
    wa_index = lax.axis_index("wa")
    share_rows = block_rows // lax.axis_size("wa")
    share_start = wa_index * share_rows
    local_width = conv_weight.shape[2]
    hidden_width = gate_up_weight.shape[3]
    in_matrix = in_weight[0].reshape(model_width, 3 * local_width)
    conv_taps = conv_weight[0]
    out_matrix = out_weight[0]
    gain_row = norm_gain[0]
    gate_up = gate_up_weight[0].reshape(model_width, 2 * hidden_width)
    down_matrix = down_weight[0]
    edge_zeros = jnp.zeros((2, local_width), jnp.bfloat16)
    received = jnp.zeros((block_rows, model_width), jnp.bfloat16)
    carried = edge_zeros
    outputs = []
    saved = []
    for step_num in range(micro_count + 1):
        micro_index = step_num - section_index
        inputs = jnp.where(section_index == 0, tokens[min(step_num, micro_count - 1)], received)
        projected = jnp.dot(inputs, in_matrix, preferred_element_type=jnp.float32).reshape(
            block_rows, 3, local_width
        )
        gated_in = (projected[:, 0] * projected[:, 2]).astype(jnp.bfloat16)
        incoming = passed_along(gated_in[block_rows - 2 :], "seq", 1)
        first_rows = jnp.where(
            seq_index == 0, jnp.where(micro_index == 0, edge_zeros, carried), incoming
        )
        carried = incoming
        padded = jnp.concatenate([first_rows, gated_in], 0).astype(jnp.float32)
        conv_out = (
            conv_taps[0] * padded[:block_rows]
            + conv_taps[1] * padded[1 : block_rows + 1]
            + conv_taps[2] * padded[2:]
        )
        mixed_in = (projected[:, 1] * conv_out).astype(jnp.bfloat16)
        mixed_sum = lax.psum(
            jnp.dot(mixed_in, out_matrix, preferred_element_type=jnp.float32), "wa"
        )
        residual = inputs.astype(jnp.float32) + mixed_sum
        inv_rms = lax.rsqrt(jnp.mean(residual * residual, -1, keepdims=True) + EPSILON)
        normed = (residual * inv_rms * gain_row).astype(jnp.bfloat16)
        gate_up_val = jnp.dot(normed, gate_up, preferred_element_type=jnp.float32).reshape(
            block_rows, 2, hidden_width
        )
        gate_val = gate_up_val[:, 0]
        up_val = gate_up_val[:, 1]
        hidden = (silu_parts(gate_val)[0] * up_val).astype(jnp.bfloat16)
        own_residual = lax.dynamic_slice_in_dim(residual, share_start, share_rows, 0)
        layer_rows = (
            own_residual
            + lax.psum_scatter(
                jnp.dot(hidden, down_matrix, preferred_element_type=jnp.float32),
                "wa",
                scatter_dimension=0,
                tiled=True,
            )
        ).astype(jnp.bfloat16)
        outputs.append(layer_rows)
        saved.append(
            (
                inputs,
                projected,
                padded,
                conv_out,
                mixed_in,
                residual,
                inv_rms,
                normed,
                gate_val,
                up_val,
                hidden,
            )
        )
        if step_num < micro_count:
            arrived = shifted(layer_rows, "section", 1)
            received = lax.all_gather(arrived, "wa", axis=0, tiled=True)
    stacked_out = jnp.stack(outputs)
    layer_block = jnp.where(section_index == 0, stacked_out[:micro_count], stacked_out[1:])
    tail_zeros = jnp.zeros((2, local_width), jnp.float32)
    received_grad = jnp.zeros((block_rows, model_width), jnp.float32)
    carried_grad = tail_zeros
    in_total = jnp.zeros((model_width, 3 * local_width), jnp.float32)
    tap_total = jnp.zeros((3, local_width), jnp.float32)
    out_total = jnp.zeros((local_width, model_width), jnp.float32)
    gain_total = jnp.zeros((model_width,), jnp.float32)
    gate_up_total = jnp.zeros((model_width, 2 * hidden_width), jnp.float32)
    down_total = jnp.zeros((hidden_width, model_width), jnp.float32)
    grad_rows = []
    for step_num in range(micro_count + 1):
        micro_index = micro_count - 1 - step_num + (1 - section_index)
        valid = (micro_index >= 0) & (micro_index < micro_count)
        (
            inputs,
            projected,
            padded,
            conv_out,
            mixed_in,
            residual,
            inv_rms,
            normed,
            gate_val,
            up_val,
            hidden,
        ) = saved[micro_count - step_num]
        out_grad = jnp.where(
            section_index == 1, cotangent[max(micro_count - 1 - step_num, 0)], received_grad
        )
        out_bf = out_grad.astype(jnp.bfloat16)
        hidden_grad = contract_last(out_bf, down_matrix)
        silu_val, silu_slope = silu_parts(gate_val)
        gate_up_bf = (
            jnp.stack([hidden_grad * up_val * silu_slope, hidden_grad * silu_val], 1)
            .astype(jnp.bfloat16)
            .reshape(block_rows, 2 * hidden_width)
        )
        normed_grad = lax.psum(
            contract_last(gate_up_bf, gate_up).astype(jnp.bfloat16), "wa"
        ).astype(jnp.float32)
        scaled_grad = normed_grad * gain_row
        gain_term = jnp.sum(normed_grad * residual * inv_rms, 0)
        residual_grad = (
            out_grad
            + inv_rms * scaled_grad
            - residual * inv_rms**3 * jnp.mean(scaled_grad * residual, -1, keepdims=True)
        )
        residual_bf = residual_grad.astype(jnp.bfloat16)
        mixed_grad = contract_last(residual_bf, out_matrix)
        c_grad = mixed_grad * conv_out
        conv_grad = mixed_grad * projected[:, 1]
        incoming_grad = passed_along(conv_grad[:2], "seq", -1)
        last_rows = jnp.where(
            seq_index == seq_count - 1,
            jnp.where(micro_index == micro_count - 1, tail_zeros, carried_grad),
            incoming_grad,
        )
        carried_grad = incoming_grad
        extended = jnp.concatenate([conv_grad, last_rows], 0)
        gated_grad = (
            conv_taps[2] * extended[:block_rows]
            + conv_taps[1] * extended[1 : block_rows + 1]
            + conv_taps[0] * extended[2:]
        )
        tap_grad = jnp.stack(
            [jnp.sum(conv_grad * padded[offset : offset + block_rows], 0) for offset in range(3)]
        )
        proj_bf = (
            jnp.stack([gated_grad * projected[:, 2], c_grad, gated_grad * projected[:, 0]], 1)
            .astype(jnp.bfloat16)
            .reshape(block_rows, 3 * local_width)
        )
        own_grad = lax.dynamic_slice_in_dim(residual_grad, share_start, share_rows, 0)
        input_rows_grad = own_grad + lax.psum_scatter(
            contract_last(proj_bf, in_matrix).astype(jnp.bfloat16),
            "wa",
            scatter_dimension=0,
            tiled=True,
        ).astype(jnp.float32)
        grad_rows.append(input_rows_grad)
        in_total = in_total + jnp.where(valid, contract_first(inputs, proj_bf), 0.0)
        tap_total = tap_total + jnp.where(valid, tap_grad, 0.0)
        out_total = out_total + jnp.where(valid, contract_first(mixed_in, residual_bf), 0.0)
        gain_total = gain_total + jnp.where(valid, gain_term, 0.0)
        gate_up_total = gate_up_total + jnp.where(valid, contract_first(normed, gate_up_bf), 0.0)
        down_total = down_total + jnp.where(valid, contract_first(hidden, out_bf), 0.0)
        if step_num < micro_count:
            arrived_grad = shifted(input_rows_grad.astype(jnp.bfloat16), "section", -1).astype(
                input_rows_grad.dtype
            )
            received_grad = lax.all_gather(
                arrived_grad.astype(jnp.bfloat16), "wa", axis=0, tiled=True
            ).astype(arrived_grad.dtype)
    stacked_grad = jnp.stack(grad_rows)
    grad_block = jnp.where(section_index == 1, stacked_grad[:micro_count], stacked_grad[1:])[::-1]
    in_sum, tap_sum, out_sum, gain_sum, gate_up_sum, down_sum = (
        lax.psum(in_total.astype(jnp.bfloat16), "seq").astype(jnp.float32),
        lax.psum(tap_total.astype(jnp.bfloat16), "seq").astype(jnp.float32),
        lax.psum(out_total.astype(jnp.bfloat16), "seq").astype(jnp.float32),
        lax.psum(gain_total.astype(jnp.bfloat16), "seq").astype(jnp.float32),
        lax.psum(gate_up_total.astype(jnp.bfloat16), "seq").astype(jnp.float32),
        lax.psum(down_total.astype(jnp.bfloat16), "seq").astype(jnp.float32),
    )
    return (
        layer_block[None],
        grad_block[None],
        in_sum.reshape(1, model_width, 3, local_width),
        tap_sum[None],
        out_sum[None],
        gain_sum[None],
        gate_up_sum.reshape(1, model_width, 2, hidden_width),
        down_sum[None],
    )


def solution(mesh):
    in_specs = (
        P(None, "seq", None),
        P(None, "seq", None),
        P("section", None, None, "wa"),
        P("section", None, "wa"),
        P("section", "wa", None),
        P("section", None),
        P("section", None, None, "wa"),
        P("section", "wa", None),
    )
    out_specs = (
        P("section", None, ("seq", "wa"), None),
        P("section", None, ("seq", "wa"), None),
        P("section", None, None, "wa"),
        P("section", None, "wa"),
        P("section", "wa", None),
        P("section", None),
        P("section", None, None, "wa"),
        P("section", "wa", None),
    )
    return jax.shard_map(body, mesh=mesh, in_specs=in_specs, out_specs=out_specs, check_vma=False)
```

profile of v0, /device:TPU:1, one launch (start us, length us, event | category | flops | bytes accessed | tf_op | source)
XLA Modules:
  0.0 2037.2 jit_solution(783066171614633669)
XLA Ops:
  16.3 88.3 %all-reduce.14.cloned.1.call-done = f32[256,1024]{1,0:T(8,128)} async-done(((f32[256,1024]{1,0:T(8,128)}), f32[256,1024]{1,0:T(8,128)}) %all-reduce.14.cloned.1.call-update) | async-done | bytes 1048592 | tf_op jit(solution)/shard_map/psum | solution.py:80
  109.4 72.1 %reduce-scatter.11.cloned.1.call-done = f32[16,1024]{1,0:T(8,128)} async-done(((f32[256,1024]{1,0:T(8,128)}), f32[16,1024]{1,0:T(8,128)}) %reduce-scatter.11.cloned.1.call-update) | async-done | bytes 65552 | tf_op jit(solution)/shard_map/reduce_scatter | solution.py:95
  186.6 18.4 all_gather.24
  213.2 88.8 %all-reduce.16.cloned.1.call-done = f32[256,1024]{1,0:T(8,128)} async-done(((f32[256,1024]{1,0:T(8,128)}), f32[256,1024]{1,0:T(8,128)}) %all-reduce.16.cloned.1.call-update) | async-done | bytes 1048592 | tf_op jit(solution)/shard_map/psum | solution.py:80
  307.0 72.1 %reduce-scatter.13.cloned.1.call-done = f32[16,1024]{1,0:T(8,128)} async-done(((f32[256,1024]{1,0:T(8,128)}), f32[16,1024]{1,0:T(8,128)}) %reduce-scatter.13.cloned.1.call-update) | async-done | bytes 65552 | tf_op jit(solution)/shard_map/reduce_scatter | solution.py:95
  384.2 18.4 all_gather.25
  416.7 88.8 %all-reduce.18.cloned.1.call-done = f32[256,1024]{1,0:T(8,128)} async-done(((f32[256,1024]{1,0:T(8,128)}), f32[256,1024]{1,0:T(8,128)}) %all-reduce.18.cloned.1.call-update) | async-done | bytes 1048592 | tf_op jit(solution)/shard_map/psum | solution.py:80
  510.7 72.1 %reduce-scatter.15.cloned.1.call-done = f32[16,1024]{1,0:T(8,128)} async-done(((f32[256,1024]{1,0:T(8,128)}), f32[16,1024]{1,0:T(8,128)}) %reduce-scatter.15.cloned.1.call-update) | async-done | bytes 65552 | tf_op jit(solution)/shard_map/reduce_scatter | solution.py:95
  588.0 18.4 all_gather.26
  620.5 88.8 %all-reduce.20.cloned.1.call-done = f32[256,1024]{1,0:T(8,128)} async-done(((f32[256,1024]{1,0:T(8,128)}), f32[256,1024]{1,0:T(8,128)}) %all-reduce.20.cloned.1.call-update) | async-done | bytes 1048592 | tf_op jit(solution)/shard_map/psum | solution.py:80
  714.5 72.2 %reduce-scatter.17.cloned.1.call-done = f32[16,1024]{1,0:T(8,128)} async-done(((f32[256,1024]{1,0:T(8,128)}), f32[16,1024]{1,0:T(8,128)}) %reduce-scatter.17.cloned.1.call-update) | async-done | bytes 65552 | tf_op jit(solution)/shard_map/reduce_scatter | solution.py:95
  791.8 18.4 all_gather.27
  824.5 88.7 %all-reduce.22.cloned.1.call-done = f32[256,1024]{1,0:T(8,128)} async-done(((f32[256,1024]{1,0:T(8,128)}), f32[256,1024]{1,0:T(8,128)}) %all-reduce.22.cloned.1.call-update) | async-done | bytes 1048592 | tf_op jit(solution)/shard_map/psum | solution.py:80
  921.0 84.7 %all-reduce.24.cloned.1.call-done = bf16[256,1024]{1,0:T(8,128)(2,1)} async-done(((bf16[256,1024]{1,0:T(8,128)(2,1)}), bf16[256,1024]{1,0:T(8,128)(2,1)}) %all-reduce.24.cloned.1.call-update) | async-done | bytes 524304 | tf_op jit(solution)/shard_map/psum | solution.py:160
  1016.2 72.9 %reduce-scatter.21.cloned.1.call-done = bf16[16,1024]{1,0:T(8,128)(2,1)} async-done(((bf16[256,1024]{1,0:T(8,128)(2,1)}), bf16[16,1024]{1,0:T(8,128)(2,1)}) %reduce-scatter.21.cloned.1.call-update) | async-done | bytes 32784 | tf_op jit(solution)/shard_map/reduce_scatter | solution.py:196
  1095.7 18.2 all_gather.28
  1118.2 87.4 %all-reduce.26.cloned.1.call-done = bf16[256,1024]{1,0:T(8,128)(2,1)} async-done(((bf16[256,1024]{1,0:T(8,128)(2,1)}), bf16[256,1024]{1,0:T(8,128)(2,1)}) %all-reduce.26.cloned.1.call-update) | async-done | bytes 524304 | tf_op jit(solution)/shard_map/psum | solution.py:160
  1216.4 72.9 %reduce-scatter.23.cloned.1.call-done = bf16[16,1024]{1,0:T(8,128)(2,1)} async-done(((bf16[256,1024]{1,0:T(8,128)(2,1)}), bf16[16,1024]{1,0:T(8,128)(2,1)}) %reduce-scatter.23.cloned.1.call-update) | async-done | bytes 32784 | tf_op jit(solution)/shard_map/reduce_scatter | solution.py:196
  1295.8 18.2 all_gather.29
  1318.4 87.5 %all-reduce.28.cloned.1.call-done = bf16[256,1024]{1,0:T(8,128)(2,1)} async-done(((bf16[256,1024]{1,0:T(8,128)(2,1)}), bf16[256,1024]{1,0:T(8,128)(2,1)}) %all-reduce.28.cloned.1.call-update) | async-done | bytes 524304 | tf_op jit(solution)/shard_map/psum | solution.py:160
  1416.5 72.9 %reduce-scatter.25.cloned.1.call-done = bf16[16,1024]{1,0:T(8,128)(2,1)} async-done(((bf16[256,1024]{1,0:T(8,128)(2,1)}), bf16[16,1024]{1,0:T(8,128)(2,1)}) %reduce-scatter.25.cloned.1.call-update) | async-done | bytes 32784 | tf_op jit(solution)/shard_map/reduce_scatter | solution.py:196
  1495.9 18.1 all_gather.30
  1518.6 87.3 %all-reduce.30.cloned.1.call-done = bf16[256,1024]{1,0:T(8,128)(2,1)} async-done(((bf16[256,1024]{1,0:T(8,128)(2,1)}), bf16[256,1024]{1,0:T(8,128)(2,1)}) %all-reduce.30.cloned.1.call-update) | async-done | bytes 524304 | tf_op jit(solution)/shard_map/psum | solution.py:160
  1617.3 71.7 %reduce-scatter.27.cloned.1.call-done = bf16[16,1024]{1,0:T(8,128)(2,1)} async-done(((bf16[256,1024]{1,0:T(8,128)(2,1)}), bf16[16,1024]{1,0:T(8,128)(2,1)}) %reduce-scatter.27.cloned.1.call-update) | async-done | bytes 32784 | tf_op jit(solution)/shard_map/reduce_scatter | solution.py:196
  1690.5 4.3 collective-permute-start.16
  1697.4 18.6 all_gather.31
  1743.4 63.0 %all-reduce.32.cloned.1.call-done = bf16[256,1024]{1,0:T(8,128)(2,1)} async-done(((bf16[256,1024]{1,0:T(8,128)(2,1)}), bf16[256,1024]{1,0:T(8,128)(2,1)}) %all-reduce.32.cloned.1.call-update) | async-done | bytes 524304 | tf_op jit(solution)/shard_map/psum | solution.py:160
  1816.5 5.9 add_convert_fusion
  1828.8 53.3 %reduce-scatter.19.cloned.1.call-done = f32[16,1024]{1,0:T(8,128)} async-done(((f32[256,1024]{1,0:T(8,128)}), f32[16,1024]{1,0:T(8,128)}) %reduce-scatter.19.cloned.1.call-update) | async-done | bytes 65552 | tf_op jit(solution)/shard_map/reduce_scatter | solution.py:95
  1883.9 8.5 all-reduce
  1893.6 63.2 %reduce-scatter.29.cloned.1.call-done = bf16[16,1024]{1,0:T(8,128)(2,1)} async-done(((bf16[256,1024]{1,0:T(8,128)(2,1)}), bf16[16,1024]{1,0:T(8,128)(2,1)}) %reduce-scatter.29.cloned.1.call-update) | async-done | bytes 32784 | tf_op jit(solution)/shard_map/reduce_scatter | solution.py:196
  1958.3 65.0 %all-reduce.34.cloned.1.call-done = (bf16[1,1024,3,64]{1,3,2,0:T(8,128)(2,1)}, bf16[1,64,1024]{2,1,0:T(8,128)(2,1)}, bf16[1,1024,2,288]{1,3,2,0:T(8,128)(2,1)}, bf16[1,288,1024]{2,1,0:T(8,128)(2,1)}) async-done(((bf16[1,1024,3,64]{1,3,2,0:T(8,128)(2,1)}, bf16[1,64,1024]{2,1,0:T(8,128)(2,1)}, bf16[1,1024,2,288]{1,3,2,0:T(8,128)(2,1)}, bf16[1,288,1024]{2,1,0:T(8,128)(2,1)}), ...) | async-done | bytes 2293776 | tf_op jit(solution)/shard_map/psum | solution.py:219
  (594 shorter events, 241.7 us)
Async XLA Ops:
  7.2 97.4 %all-reduce.14.cloned.1.call-start = ((), (), s32[]{:S(2)}) async-start(), calls=%async_computation.10 | async-start | bytes 2097152 | tf_op jit(solution)/shard_map/psum | solution.py:80
  8.9 4.4 collective-permute-start
  16.2 165.3 %reduce-scatter.11.cloned.1.call-start = ((), (), s32[]{:S(2)}) async-start(), calls=%async_computation.11 | async-start | bytes 1114112 | tf_op jit(solution)/shard_map/reduce_scatter | solution.py:95
  109.4 192.6 %all-reduce.16.cloned.1.call-start = ((), (), s32[]{:S(2)}) async-start(), calls=%async_computation.12 | async-start | bytes 2097152 | tf_op jit(solution)/shard_map/psum | solution.py:80
  182.4 4.2 collective-permute-start.1
  213.1 166.0 %reduce-scatter.13.cloned.1.call-start = ((), (), s32[]{:S(2)}) async-start(), calls=%async_computation.13 | async-start | bytes 1114112 | tf_op jit(solution)/shard_map/reduce_scatter | solution.py:95
  307.0 198.6 %all-reduce.18.cloned.1.call-start = ((), (), s32[]{:S(2)}) async-start(), calls=%async_computation.14 | async-start | bytes 2097152 | tf_op jit(solution)/shard_map/psum | solution.py:80
  380.0 4.3 collective-permute-start.3
  406.9 4.1 collective-permute-start.4
  416.7 166.2 %reduce-scatter.15.cloned.1.call-start = ((), (), s32[]{:S(2)}) async-start(), calls=%async_computation.15 | async-start | bytes 1114112 | tf_op jit(solution)/shard_map/reduce_scatter | solution.py:95
  510.7 198.6 %all-reduce.20.cloned.1.call-start = ((), (), s32[]{:S(2)}) async-start(), calls=%async_computation.16 | async-start | bytes 2097152 | tf_op jit(solution)/shard_map/psum | solution.py:80
  583.8 4.2 collective-permute-start.5
  610.6 4.1 collective-permute-start.6
  620.4 166.3 %reduce-scatter.17.cloned.1.call-start = ((), (), s32[]{:S(2)}) async-start(), calls=%async_computation.17 | async-start | bytes 1114112 | tf_op jit(solution)/shard_map/reduce_scatter | solution.py:95
  714.5 198.7 %all-reduce.22.cloned.1.call-start = ((), (), s32[]{:S(2)}) async-start(), calls=%async_computation.18 | async-start | bytes 2097152 | tf_op jit(solution)/shard_map/psum | solution.py:80
  787.6 4.2 collective-permute-start.7
  824.2 181.5 %all-reduce.24.cloned.1.call-start = ((), (), s32[]{:S(2)}) async-start(), calls=%async_computation.20 | async-start | bytes 1048576 | tf_op jit(solution)/shard_map/psum | solution.py:160
  921.0 168.2 %reduce-scatter.21.cloned.1.call-start = ((), (), s32[]{:S(2)}) async-start(), calls=%async_computation.21 | async-start | bytes 557056 | tf_op jit(solution)/shard_map/reduce_scatter | solution.py:196
  1016.2 189.4 %all-reduce.26.cloned.1.call-start = ((), (), s32[]{:S(2)}) async-start(), calls=%async_computation.22 | async-start | bytes 1048576 | tf_op jit(solution)/shard_map/psum | solution.py:160
  1090.7 5.0 collective-permute-start.10
  1118.1 171.2 %reduce-scatter.23.cloned.1.call-start = ((), (), s32[]{:S(2)}) async-start(), calls=%async_computation.23 | async-start | bytes 557056 | tf_op jit(solution)/shard_map/reduce_scatter | solution.py:196
  1216.3 189.5 %all-reduce.28.cloned.1.call-start = ((), (), s32[]{:S(2)}) async-start(), calls=%async_computation.24 | async-start | bytes 1048576 | tf_op jit(solution)/shard_map/psum | solution.py:160
  1290.8 5.0 collective-permute-start.12
  1318.3 171.1 %reduce-scatter.25.cloned.1.call-start = ((), (), s32[]{:S(2)}) async-start(), calls=%async_computation.25 | async-start | bytes 557056 | tf_op jit(solution)/shard_map/reduce_scatter | solution.py:196
  1416.5 189.4 %all-reduce.30.cloned.1.call-start = ((), (), s32[]{:S(2)}) async-start(), calls=%async_computation.26 | async-start | bytes 1048576 | tf_op jit(solution)/shard_map/psum | solution.py:160
  1490.9 5.0 collective-permute-start.14
  1518.4 170.7 %reduce-scatter.27.cloned.1.call-start = ((), (), s32[]{:S(2)}) async-start(), calls=%async_computation.27 | async-start | bytes 557056 | tf_op jit(solution)/shard_map/reduce_scatter | solution.py:196
  1616.0 190.4 %all-reduce.32.cloned.1.call-start = ((), (), s32[]{:S(2)}) async-start(), calls=%async_computation.28 | async-start | bytes 1048576 | tf_op jit(solution)/shard_map/psum | solution.py:160
  1690.5 6.9 collective-permute-start.16
  1720.0 162.1 %reduce-scatter.19.cloned.1.call-start = ((), (), s32[]{:S(2)}) async-start(), calls=%async_computation.19 | async-start | bytes 1114112 | tf_op jit(solution)/shard_map/reduce_scatter | solution.py:95
  1725.9 230.9 %reduce-scatter.29.cloned.1.call-start = ((), (), s32[]{:S(2)}) async-start(), calls=%async_computation.29 | async-start | bytes 557056 | tf_op jit(solution)/shard_map/reduce_scatter | solution.py:196
  1816.2 207.2 %all-reduce.34.cloned.1.call-start = ((), (), s32[]{:S(2)}) async-start(), calls=%async_computation.30 | async-start | bytes 4587520 | tf_op jit(solution)/shard_map/psum | solution.py:219
  (180 other events, 2752.4 us)
Sparse Core Ops, SparseCore 0:
  16.3 88.1 all-reduce.13
  109.5 72.0 reduce-scatter.10
  213.3 88.7 all-reduce.15
  307.1 71.9 reduce-scatter.12
  416.8 88.6 all-reduce.17
  510.8 72.0 reduce-scatter.14
  620.6 88.7 all-reduce.19
  714.6 72.0 reduce-scatter.16
  824.3 88.7 all-reduce.21
  921.1 84.5 all-reduce.23
  1016.3 72.8 reduce-scatter.20
  1118.3 87.3 all-reduce.25
  1216.4 72.8 reduce-scatter.22
  1318.4 87.3 all-reduce.27
  1416.6 72.8 reduce-scatter.24
  1518.5 87.3 all-reduce.29
  1616.2 72.8 reduce-scatter.26
  1720.1 86.2 all-reduce.31
  1809.9 72.0 reduce-scatter.18
  1885.1 71.6 reduce-scatter.28
  1960.1 63.1 all-reduce.33
where the time goes:
time: 2040 us
  waiting for transfers between devices  1650 us (81%)
  blocking collectives  155 us (8%)
  matrix products  81.4 us (4%)
  other arithmetic  67.3 us (3%)
  starting transfers between devices  42.4 us (2%)
  local copies, waits for them, and re-layouts  28.3 us (1%)
    psum x5, waiting for transfers between devices, body(): lax.psum(jnp.dot(mixed_in, out_matrix, preferred_element_type=jnp.float32...  443 us
    psum x5, waiting for transfers between devices, body(): lax.psum(contract_last(gate_up_bf, gate_up).astype(jnp.bfloat16), 'wa')  410 us
    reduce_scatter x5, waiting for transfers between devices, body(): lax.psum_scatter(contract_last(proj_bf, in_matrix).astype(jnp.bfloat16),...  354 us
    reduce_scatter x5, waiting for transfers between devices, body(): lax.psum_scatter(jnp.dot(hidden, down_matrix, preferred_element_type=jnp....  342 us
    all_gather x4, blocking collectives, body(): received = lax.all_gather(arrived, 'wa', axis=0, tiled=True)  73.5 us
    all_gather x4, blocking collectives, body(): lax.all_gather(arrived_grad.astype(jnp.bfloat16), 'wa', axis=0, tiled=True)  73.1 us
    psum x1, waiting for transfers between devices, body(): lax.psum(in_total.astype(jnp.bfloat16), 'seq').astype(jnp.float32)  65 us
  transfers between devices with their start and end apart: 39, of which 37 were waited for; matrix products, arithmetic and copies ran while one was open for 2% of the time, Pallas kernels for 0%

commit v1 on v0

--- a/solution.py
+++ b/solution.py
@@ -117,7 +117,16 @@
         )
         if step_num < micro_count:
             arrived = shifted(layer_rows, "section", 1)
-            received = lax.all_gather(arrived, "wa", axis=0, tiled=True)
+            ring = [arrived]
+            for hop in range(15):
+                ring.append(
+                    lax.ppermute(ring[-1], "wa", [(dev, (dev + 1) % 16) for dev in range(16)])
+                )
+            received = jnp.roll(
+                jnp.concatenate(ring[::-1], axis=0),
+                (lax.axis_index("wa") + 1) * ring[0].shape[0],
+                axis=0,
+            )
     stacked_out = jnp.stack(outputs)
     layer_block = jnp.where(section_index == 0, stacked_out[:micro_count], stacked_out[1:])
     tail_zeros = jnp.zeros((2, local_width), jnp.float32)

time: 2040 us -> 2380 us (1.17)
  waiting for transfers between devices: 1650 us -> 2050 us
  blocking collectives: 155 us -> 81.6 us
    ppermute x0 -> x60, waiting for transfers between devices: none -> 363 us  [body(): lax.ppermute(ring[-1], 'wa', [(dev, (dev + 1) % 16) for dev in range(16)])]
    all_gather x4 -> x0, blocking collectives: 73.5 us -> none  [body(): received = lax.all_gather(arrived, 'wa', axis=0, tiled=True)]
    psum x5, waiting for transfers between devices: 443 us -> 481 us  [body(): lax.psum(jnp.dot(mixed_in, out_matrix, preferred_element_type=jnp.float32...]
  transfers between devices with their start and end apart: 39 -> 99, of which waited for: 37 -> 97; matrix products, arithmetic and copies ran while one was open for 2% -> 2% of each run, Pallas kernels for 0% -> 0%
where the time goes in v1:
time: 2380 us; the launch traced here: 2370 us
  waiting for transfers between devices  2050 us (86%)
  blocking collectives  81.6 us (3%)
  matrix products  81.5 us (3%)
  other arithmetic  69.5 us (3%)
  starting transfers between devices  46.9 us (2%)
  local copies, waits for them, and re-layouts  28.7 us (1%)
    psum x5, waiting for transfers between devices, body(): lax.psum(jnp.dot(mixed_in, out_matrix, preferred_element_type=jnp.float32...  481 us
    psum x5, waiting for transfers between devices, body(): lax.psum(contract_last(gate_up_bf, gate_up).astype(jnp.bfloat16), 'wa')  410 us
    ppermute x60, waiting for transfers between devices, body(): lax.ppermute(ring[-1], 'wa', [(dev, (dev + 1) % 16) for dev in range(16)])  363 us
    reduce_scatter x5, waiting for transfers between devices, body(): lax.psum_scatter(contract_last(proj_bf, in_matrix).astype(jnp.bfloat16),...  354 us
    reduce_scatter x5, waiting for transfers between devices, body(): lax.psum_scatter(jnp.dot(hidden, down_matrix, preferred_element_type=jnp....  341 us
    all_gather x4, blocking collectives, body(): lax.all_gather(arrived_grad.astype(jnp.bfloat16), 'wa', axis=0, tiled=True)  73 us
    psum x1, waiting for transfers between devices, body(): lax.psum(in_total.astype(jnp.bfloat16), 'seq').astype(jnp.float32)  65.1 us
  transfers between devices with their start and end apart: 99, of which 97 were waited for; matrix products, arithmetic and copies ran while one was open for 2% of the time, Pallas kernels for 0%

profile of v1, /device:TPU:1, one launch (start us, length us, event | category | flops | bytes accessed | tf_op | source)
XLA Modules:
  0.0 2372.5 jit_solution(10258096485236485752)
XLA Ops:
  15.6 88.3 %all-reduce.14.cloned.1.call-done = f32[256,1024]{1,0:T(8,128)} async-done(((f32[256,1024]{1,0:T(8,128)}), f32[256,1024]{1,0:T(8,128)}) %all-reduce.14.cloned.1.call-update) | async-done | bytes 1048592 | tf_op jit(solution)/shard_map/psum | solution.py:80
  108.8 72.1 %reduce-scatter.11.cloned.1.call-done = f32[16,1024]{1,0:T(8,128)} async-done(((f32[256,1024]{1,0:T(8,128)}), f32[16,1024]{1,0:T(8,128)}) %reduce-scatter.11.cloned.1.call-update) | async-done | bytes 65552 | tf_op jit(solution)/shard_map/reduce_scatter | solution.py:95
  222.5 6.4 collective-permute-done.8
  259.4 6.1 collective-permute-done.14
  286.6 98.5 %all-reduce.16.cloned.1.call-done = f32[256,1024]{1,0:T(8,128)} async-done(((f32[256,1024]{1,0:T(8,128)}), f32[256,1024]{1,0:T(8,128)}) %all-reduce.16.cloned.1.call-update) | async-done | bytes 1048592 | tf_op jit(solution)/shard_map/psum | solution.py:80
  390.1 72.2 %reduce-scatter.13.cloned.1.call-done = f32[16,1024]{1,0:T(8,128)} async-done(((f32[256,1024]{1,0:T(8,128)}), f32[16,1024]{1,0:T(8,128)}) %reduce-scatter.13.cloned.1.call-update) | async-done | bytes 65552 | tf_op jit(solution)/shard_map/reduce_scatter | solution.py:95
  504.0 6.4 collective-permute-done.25
  540.9 6.1 collective-permute-done.31
  574.2 98.3 %all-reduce.18.cloned.1.call-done = f32[256,1024]{1,0:T(8,128)} async-done(((f32[256,1024]{1,0:T(8,128)}), f32[256,1024]{1,0:T(8,128)}) %all-reduce.18.cloned.1.call-update) | async-done | bytes 1048592 | tf_op jit(solution)/shard_map/psum | solution.py:80
  677.7 72.1 %reduce-scatter.15.cloned.1.call-done = f32[16,1024]{1,0:T(8,128)} async-done(((f32[256,1024]{1,0:T(8,128)}), f32[16,1024]{1,0:T(8,128)}) %reduce-scatter.15.cloned.1.call-update) | async-done | bytes 65552 | tf_op jit(solution)/shard_map/reduce_scatter | solution.py:95
  791.4 6.4 collective-permute-done.42
  862.1 98.3 %all-reduce.20.cloned.1.call-done = f32[256,1024]{1,0:T(8,128)} async-done(((f32[256,1024]{1,0:T(8,128)}), f32[256,1024]{1,0:T(8,128)}) %all-reduce.20.cloned.1.call-update) | async-done | bytes 1048592 | tf_op jit(solution)/shard_map/psum | solution.py:80
  965.6 72.1 %reduce-scatter.17.cloned.1.call-done = f32[16,1024]{1,0:T(8,128)} async-done(((f32[256,1024]{1,0:T(8,128)}), f32[16,1024]{1,0:T(8,128)}) %reduce-scatter.17.cloned.1.call-update) | async-done | bytes 65552 | tf_op jit(solution)/shard_map/reduce_scatter | solution.py:95
  1079.4 6.4 collective-permute-done.59
  1149.7 98.1 %all-reduce.22.cloned.1.call-done = f32[256,1024]{1,0:T(8,128)} async-done(((f32[256,1024]{1,0:T(8,128)}), f32[256,1024]{1,0:T(8,128)}) %all-reduce.22.cloned.1.call-update) | async-done | bytes 1048592 | tf_op jit(solution)/shard_map/psum | solution.py:80
  1255.7 84.7 %all-reduce.24.cloned.1.call-done = bf16[256,1024]{1,0:T(8,128)(2,1)} async-done(((bf16[256,1024]{1,0:T(8,128)(2,1)}), bf16[256,1024]{1,0:T(8,128)(2,1)}) %all-reduce.24.cloned.1.call-update) | async-done | bytes 524304 | tf_op jit(solution)/shard_map/psum | solution.py:169
  1351.0 72.9 %reduce-scatter.21.cloned.1.call-done = bf16[16,1024]{1,0:T(8,128)(2,1)} async-done(((bf16[256,1024]{1,0:T(8,128)(2,1)}), bf16[16,1024]{1,0:T(8,128)(2,1)}) %reduce-scatter.21.cloned.1.call-update) | async-done | bytes 32784 | tf_op jit(solution)/shard_map/reduce_scatter | solution.py:205
  1430.4 18.2 all_gather.12
  1452.9 87.5 %all-reduce.26.cloned.1.call-done = bf16[256,1024]{1,0:T(8,128)(2,1)} async-done(((bf16[256,1024]{1,0:T(8,128)(2,1)}), bf16[256,1024]{1,0:T(8,128)(2,1)}) %all-reduce.26.cloned.1.call-update) | async-done | bytes 524304 | tf_op jit(solution)/shard_map/psum | solution.py:169
  1551.1 72.9 %reduce-scatter.23.cloned.1.call-done = bf16[16,1024]{1,0:T(8,128)(2,1)} async-done(((bf16[256,1024]{1,0:T(8,128)(2,1)}), bf16[16,1024]{1,0:T(8,128)(2,1)}) %reduce-scatter.23.cloned.1.call-update) | async-done | bytes 32784 | tf_op jit(solution)/shard_map/reduce_scatter | solution.py:205
  1630.6 18.1 all_gather.13
  1653.1 87.5 %all-reduce.28.cloned.1.call-done = bf16[256,1024]{1,0:T(8,128)(2,1)} async-done(((bf16[256,1024]{1,0:T(8,128)(2,1)}), bf16[256,1024]{1,0:T(8,128)(2,1)}) %all-reduce.28.cloned.1.call-update) | async-done | bytes 524304 | tf_op jit(solution)/shard_map/psum | solution.py:169
  1751.3 72.9 %reduce-scatter.25.cloned.1.call-done = bf16[16,1024]{1,0:T(8,128)(2,1)} async-done(((bf16[256,1024]{1,0:T(8,128)(2,1)}), bf16[16,1024]{1,0:T(8,128)(2,1)}) %reduce-scatter.25.cloned.1.call-update) | async-done | bytes 32784 | tf_op jit(solution)/shard_map/reduce_scatter | solution.py:205
  1830.7 18.1 all_gather.14
  1853.4 87.3 %all-reduce.30.cloned.1.call-done = bf16[256,1024]{1,0:T(8,128)(2,1)} async-done(((bf16[256,1024]{1,0:T(8,128)(2,1)}), bf16[256,1024]{1,0:T(8,128)(2,1)}) %all-reduce.30.cloned.1.call-update) | async-done | bytes 524304 | tf_op jit(solution)/shard_map/psum | solution.py:169
  1952.1 71.8 %reduce-scatter.27.cloned.1.call-done = bf16[16,1024]{1,0:T(8,128)(2,1)} async-done(((bf16[256,1024]{1,0:T(8,128)(2,1)}), bf16[16,1024]{1,0:T(8,128)(2,1)}) %reduce-scatter.27.cloned.1.call-update) | async-done | bytes 32784 | tf_op jit(solution)/shard_map/reduce_scatter | solution.py:205
  2032.2 18.6 all_gather.15
  2078.3 63.0 %all-reduce.32.cloned.1.call-done = bf16[256,1024]{1,0:T(8,128)(2,1)} async-done(((bf16[256,1024]{1,0:T(8,128)(2,1)}), bf16[256,1024]{1,0:T(8,128)(2,1)}) %all-reduce.32.cloned.1.call-update) | async-done | bytes 524304 | tf_op jit(solution)/shard_map/psum | solution.py:169
  2164.3 52.6 %reduce-scatter.19.cloned.1.call-done = f32[16,1024]{1,0:T(8,128)} async-done(((f32[256,1024]{1,0:T(8,128)}), f32[16,1024]{1,0:T(8,128)}) %reduce-scatter.19.cloned.1.call-update) | async-done | bytes 65552 | tf_op jit(solution)/shard_map/reduce_scatter | solution.py:95
  2218.7 8.5 all-reduce
  2228.4 63.1 %reduce-scatter.29.cloned.1.call-done = bf16[16,1024]{1,0:T(8,128)(2,1)} async-done(((bf16[256,1024]{1,0:T(8,128)(2,1)}), bf16[16,1024]{1,0:T(8,128)(2,1)}) %reduce-scatter.29.cloned.1.call-update) | async-done | bytes 32784 | tf_op jit(solution)/shard_map/reduce_scatter | solution.py:205
  2293.0 65.1 %all-reduce.34.cloned.1.call-done = (bf16[1,1024,3,64]{1,3,2,0:T(8,128)(2,1)}, bf16[1,64,1024]{2,1,0:T(8,128)(2,1)}, bf16[1,1024,2,288]{1,3,2,0:T(8,128)(2,1)}, bf16[1,288,1024]{2,1,0:T(8,128)(2,1)}) async-done(((bf16[1,1024,3,64]{1,3,2,0:T(8,128)(2,1)}, bf16[1,64,1024]{2,1,0:T(8,128)(2,1)}, bf16[1,1024,2,288]{1,3,2,0:T(8,128)(2,1)}, bf16[1,288,1024]{2,1,0:T(8,128)(2,1)}), ...) | async-done | bytes 2293776 | tf_op jit(solution)/shard_map/psum | solution.py:228
  (776 shorter events, 584.3 us)
Async XLA Ops:
  7.2 96.8 %all-reduce.14.cloned.1.call-start = ((), (), s32[]{:S(2)}) async-start(), calls=%async_computation.10 | async-start | bytes 2097152 | tf_op jit(solution)/shard_map/psum | solution.py:80
  15.6 165.3 %reduce-scatter.11.cloned.1.call-start = ((), (), s32[]{:S(2)}) async-start(), calls=%async_computation.11 | async-start | bytes 1114112 | tf_op jit(solution)/shard_map/reduce_scatter | solution.py:95
  108.8 276.3 %all-reduce.16.cloned.1.call-start = ((), (), s32[]{:S(2)}) async-start(), calls=%async_computation.12 | async-start | bytes 2097152 | tf_op jit(solution)/shard_map/psum | solution.py:80
  222.5 6.4 collective-permute-start.8
  229.0 6.1 collective-permute-start.9
  259.4 6.1 collective-permute-start.14
  286.6 175.7 %reduce-scatter.13.cloned.1.call-start = ((), (), s32[]{:S(2)}) async-start(), calls=%async_computation.13 | async-start | bytes 1114112 | tf_op jit(solution)/shard_map/reduce_scatter | solution.py:95
  390.0 282.5 %all-reduce.18.cloned.1.call-start = ((), (), s32[]{:S(2)}) async-start(), calls=%async_computation.14 | async-start | bytes 2097152 | tf_op jit(solution)/shard_map/psum | solution.py:80
  479.5 6.3 collective-permute-start.21
  504.0 6.4 collective-permute-start.25
  540.9 6.1 collective-permute-start.31
  574.2 175.6 %reduce-scatter.15.cloned.1.call-start = ((), (), s32[]{:S(2)}) async-start(), calls=%async_computation.15 | async-start | bytes 1114112 | tf_op jit(solution)/shard_map/reduce_scatter | solution.py:95
  677.6 282.8 %all-reduce.20.cloned.1.call-start = ((), (), s32[]{:S(2)}) async-start(), calls=%async_computation.16 | async-start | bytes 2097152 | tf_op jit(solution)/shard_map/psum | solution.py:80
  791.4 6.4 collective-permute-start.42
  828.3 6.5 collective-permute-start.48
  862.0 175.7 %reduce-scatter.17.cloned.1.call-start = ((), (), s32[]{:S(2)}) async-start(), calls=%async_computation.17 | async-start | bytes 1114112 | tf_op jit(solution)/shard_map/reduce_scatter | solution.py:95
  965.6 282.3 %all-reduce.22.cloned.1.call-start = ((), (), s32[]{:S(2)}) async-start(), calls=%async_computation.18 | async-start | bytes 2097152 | tf_op jit(solution)/shard_map/psum | solution.py:80
  1079.4 6.4 collective-permute-start.59
  1116.2 6.1 collective-permute-start.65
  1149.5 190.9 %all-reduce.24.cloned.1.call-start = ((), (), s32[]{:S(2)}) async-start(), calls=%async_computation.20 | async-start | bytes 1048576 | tf_op jit(solution)/shard_map/psum | solution.py:169
  1255.7 168.2 %reduce-scatter.21.cloned.1.call-start = ((), (), s32[]{:S(2)}) async-start(), calls=%async_computation.21 | async-start | bytes 557056 | tf_op jit(solution)/shard_map/reduce_scatter | solution.py:205
  1350.9 189.5 %all-reduce.26.cloned.1.call-start = ((), (), s32[]{:S(2)}) async-start(), calls=%async_computation.22 | async-start | bytes 1048576 | tf_op jit(solution)/shard_map/psum | solution.py:169
  1452.9 171.2 %reduce-scatter.23.cloned.1.call-start = ((), (), s32[]{:S(2)}) async-start(), calls=%async_computation.23 | async-start | bytes 557056 | tf_op jit(solution)/shard_map/reduce_scatter | solution.py:205
  1551.1 189.5 %all-reduce.28.cloned.1.call-start = ((), (), s32[]{:S(2)}) async-start(), calls=%async_computation.24 | async-start | bytes 1048576 | tf_op jit(solution)/shard_map/psum | solution.py:169
  1653.0 171.2 %reduce-scatter.25.cloned.1.call-start = ((), (), s32[]{:S(2)}) async-start(), calls=%async_computation.25 | async-start | bytes 557056 | tf_op jit(solution)/shard_map/reduce_scatter | solution.py:205
  1751.3 189.5 %all-reduce.30.cloned.1.call-start = ((), (), s32[]{:S(2)}) async-start(), calls=%async_computation.26 | async-start | bytes 1048576 | tf_op jit(solution)/shard_map/psum | solution.py:169
  1853.2 170.7 %reduce-scatter.27.cloned.1.call-start = ((), (), s32[]{:S(2)}) async-start(), calls=%async_computation.27 | async-start | bytes 557056 | tf_op jit(solution)/shard_map/reduce_scatter | solution.py:205
  1950.8 190.4 %all-reduce.32.cloned.1.call-start = ((), (), s32[]{:S(2)}) async-start(), calls=%async_computation.28 | async-start | bytes 1048576 | tf_op jit(solution)/shard_map/psum | solution.py:169
  2025.3 6.9 collective-permute-start.76
  2054.8 162.1 %reduce-scatter.19.cloned.1.call-start = ((), (), s32[]{:S(2)}) async-start(), calls=%async_computation.19 | async-start | bytes 1114112 | tf_op jit(solution)/shard_map/reduce_scatter | solution.py:95
  2060.7 230.8 %reduce-scatter.29.cloned.1.call-start = ((), (), s32[]{:S(2)}) async-start(), calls=%async_computation.29 | async-start | bytes 557056 | tf_op jit(solution)/shard_map/reduce_scatter | solution.py:205
  2151.6 206.5 %all-reduce.34.cloned.1.call-start = ((), (), s32[]{:S(2)}) async-start(), calls=%async_computation.30 | async-start | bytes 4587520 | tf_op jit(solution)/shard_map/psum | solution.py:228
  (241 other events, 3359.3 us)
Sparse Core Ops, SparseCore 0:
  15.7 88.2 all-reduce.13
  108.9 71.9 reduce-scatter.10
  286.7 98.3 all-reduce.15
  390.1 72.0 reduce-scatter.12
  574.3 98.1 all-reduce.17
  677.7 71.9 reduce-scatter.14
  862.2 98.1 all-reduce.19
  965.7 72.0 reduce-scatter.16
  1149.6 98.1 all-reduce.21
  1255.8 84.5 all-reduce.23
  1351.0 72.8 reduce-scatter.20
  1453.0 87.3 all-reduce.25
  1551.2 72.8 reduce-scatter.22
  1653.2 87.3 all-reduce.27
  1751.4 72.7 reduce-scatter.24
  1853.3 87.3 all-reduce.29
  1951.0 72.8 reduce-scatter.26
  2054.9 86.3 all-reduce.31
  2144.8 72.0 reduce-scatter.18
  2219.9 71.5 reduce-scatter.28
  2294.9 63.2 all-reduce.33
